TPU v7x, 32 devices: a whole 2x2x4 slice. The times are simulated.
32 devices in a mesh: tm: 4 (over y, x), grid: 8 (over z, core).
Axes of the slice: x: 2, y: 2, z: 4, core: 2. Of those that a mesh axis runs over, the one named last changes fastest.
Arguments:
- clocked_seawarmth: bfloat16 [4096, 24576], P(('tm', 'grid')), may hold values from -12 to 12
- clocked_precipitation: bfloat16 [4096, 24576], P(('tm', 'grid')), may hold values from -12 to 12
- fading_weights: float32 [2, 4096], P(None, 'tm'), may hold values from 0.4 to 1, as said below
- starting_average: float32 [2, 24576], P(None, 'grid'), may hold values from -6 to 6
- warmth_random_operator: bfloat16 [24576, 256], P('grid'), may hold values from -0.0390625 to 0.0390625
- wetness_random_operator: bfloat16 [24576, 256], P('grid'), may hold values from -0.0390625 to 0.0390625
Outputs:
- warmth_summary: float32 [256, 24576], P('tm', 'grid')
- wetness_summary: float32 [256, 24576], P('tm', 'grid')
- kernel_middle: float32 [256, 256], replicated
Inputs may be any that keep to these rules, and one draw needn't show every extreme that they name: `fading_weights`: each factor lies below one.
All inputs are finite; a program needn't handle non-finite values.
Results may differ from a plain program's by a relative error of at most 0.0085.
Values may be sent and summed in bfloat16 or wider, within the bound.
A program may use at most 192 MiB of HBM per device.

v0:
```python
import jax
import jax.numpy as jnp
from jax import lax
from jax.sharding import PartitionSpec as P

BLK = 128


def carried_in(value, axis, join, neutral):
    count, mine = (lax.axis_size(axis), lax.axis_index(axis))
    pieces = jax.tree.map(lambda part: lax.all_gather(part, axis), value)
    so_far = jax.tree.map(
        lambda part, zero: jnp.full_like(part, 0) + jnp.asarray(zero, part.dtype), value, neutral
    )

    def lap(position, so_far):
        longer = join(so_far, jax.tree.map(lambda part: part[position], pieces))
        return jax.tree.map(lambda new, old: jnp.where(position < mine, new, old), longer, so_far)

    return lax.fori_loop(0, count - 1, lap, so_far)


def compose(earlier, later):
    gain_early, offset_early = earlier
    gain_late, offset_late = later
    return (gain_early * gain_late, gain_late[:, None] * offset_early + offset_late)


def reduce_line_couples(left, right):
    return lax.dot_general(
        left, right, (((0,), (0,)), ((), ())), preferred_element_type=jnp.float32
    )


def split_three(weights):
    high_part = weights.astype(jnp.bfloat16)
    rest_one = weights - high_part.astype(jnp.float32)
    middle_part = rest_one.astype(jnp.bfloat16)
    rest_two = rest_one - middle_part.astype(jnp.float32)
    return (high_part, middle_part, rest_two.astype(jnp.bfloat16))


def per_device(
    clocked_seawarmth,
    clocked_precipitation,
    fading_weights,
    starting_average,
    warmth_random_operator,
    wetness_random_operator,
):
    piled_quantities = jnp.stack([clocked_seawarmth, clocked_precipitation])
    fields = lax.all_to_all(piled_quantities, "grid", split_axis=2, concat_axis=1, tiled=True)
    hour_count = fields.shape[1]
    tile_width = fields.shape[2]
    block_count = hour_count // BLK
    decay_blocks = fading_weights.reshape(2, block_count, BLK)
    log_decay = jnp.log(decay_blocks)
    inclusive = jnp.cumsum(log_decay, axis=2)
    exclusive = inclusive - log_decay
    row_index = lax.broadcasted_iota(jnp.int32, (BLK, BLK), 0)
    col_index = lax.broadcasted_iota(jnp.int32, (BLK, BLK), 1)
    strictly = row_index > col_index
    spread = exclusive[..., :, None] - inclusive[..., None, :]
    within = (
        jnp.where(strictly, jnp.exp(jnp.minimum(spread, 0.0)), 0.0)
        * (1.0 - decay_blocks)[..., None, :]
    )
    to_end = jnp.exp(inclusive[..., -1:] - inclusive) * (1.0 - decay_blocks)
    block_gain = jnp.exp(inclusive[..., -1])
    field_blocks = fields.reshape(2, block_count, BLK, tile_width)
    inside = jnp.zeros((2, block_count, BLK, tile_width), jnp.float32)
    for within_part in split_three(within):
        inside = inside + jnp.einsum(
            "fbij,fbjp->fbip", within_part, field_blocks, preferred_element_type=jnp.float32
        )
    block_end = jnp.zeros((2, block_count, tile_width), jnp.float32)
    for to_end_part in split_three(to_end):
        block_end = block_end + jnp.einsum(
            "fbj,fbjp->fbp", to_end_part, field_blocks, preferred_element_type=jnp.float32
        )

    def fold(running, single_tick_feed):
        gain_step, end_step = single_tick_feed
        gain_now, offset_now = running
        return (
            (gain_now * gain_step, gain_step[:, None] * offset_now + end_step),
            (gain_now, offset_now),
        )

    ones_pair = jnp.ones((2,), jnp.float32)
    zero_state = jnp.zeros((2, tile_width), jnp.float32)
    device_state, entering = lax.scan(
        fold, (ones_pair, zero_state), (jnp.transpose(block_gain), jnp.moveaxis(block_end, 1, 0))
    )
    enter_gain, enter_offset = entering
    prior_gain, prior_offset = carried_in(device_state, "tm", compose, (ones_pair, zero_state))
    start_mean = prior_gain[:, None] * starting_average + prior_offset
    block_mean = jnp.moveaxis(enter_offset + enter_gain[..., None] * start_mean[None], 0, 1)
    previous = inside + jnp.exp(exclusive)[..., None] * block_mean[:, :, None, :]
    departure_amount = (
        (field_blocks.astype(jnp.float32) - previous)
        .astype(jnp.bfloat16)
        .reshape(2, hour_count, tile_width)
    )
    partials = jnp.stack(
        [
            jnp.dot(
                departure_amount[0], warmth_random_operator, preferred_element_type=jnp.float32
            ),
            jnp.dot(
                departure_amount[1], wetness_random_operator, preferred_element_type=jnp.float32
            ),
        ]
    )
    shares = lax.psum_scatter(partials, "grid", scatter_dimension=1, tiled=True).astype(
        jnp.bfloat16
    )
    compressed_lines = lax.all_gather(shares, "grid", axis=1, tiled=True)
    divisor_magnitude = (hour_count * lax.axis_size("tm")) ** (-0.5)
    warmth_lanes = compressed_lines[0]
    wetness_lanes = compressed_lines[1]
    onto_warmth = reduce_line_couples(wetness_lanes, departure_amount[0])
    onto_wetness = reduce_line_couples(warmth_lanes, departure_amount[1])
    accumulated_aggregate = lax.psum_scatter(
        jnp.stack([onto_warmth, onto_wetness], axis=1), "tm", scatter_dimension=0, tiled=True
    )
    warmth_summary = accumulated_aggregate[:, 0] * divisor_magnitude
    wetness_summary = accumulated_aggregate[:, 1] * divisor_magnitude
    cross_part = reduce_line_couples(compressed_lines[0], compressed_lines[1])
    kernel_middle = lax.psum(cross_part, "tm") * divisor_magnitude
    return (warmth_summary, wetness_summary, kernel_middle)


def solution(mesh):
    return jax.shard_map(
        per_device,
        mesh=mesh,
        in_specs=(
            P(("tm", "grid"), None),
            P(("tm", "grid"), None),
            P(None, "tm"),
            P(None, "grid"),
            P("grid", None),
            P("grid", None),
        ),
        out_specs=(P("tm", "grid"), P("tm", "grid"), P()),
        check_vma=False,
    )
```

profile of v0, /device:TPU:0, one launch (start us, length us, event | category | flops | bytes accessed | tf_op | source)
XLA Modules:
  0.0 691.9 jit_solution(17345149492004005603)
XLA Ops:
  7.2 0.0 copy-start
  7.2 10.5 %pad_maximum_fusion = bf16[2,128,24576]{2,1,0:T(8,128)(2,1)} fusion(bf16[1,128,24576]{2,1,0:T(8,128)(2,1)} %bitcast.108, bf16[1,128,24576]{2,1,0:T(8,128)(2,1)} %bitcast.109), kind=kLoop, calls=%fused_computation.14 | loop fusion | flops 6291456 | bytes 25165824 | tf_op jit(solution)/shard_map/stack | solution.py:51
  17.7 31.0 %copy.22 = bf16[2,128,24576]{1,0,2:T(2,128)(2,1)} copy(bf16[2,128,24576]{2,1,0:T(8,128)(2,1)} %pad_maximum_fusion) | data formatting | bytes 25165824 | tf_op jit(solution)/shard_map/stack | solution.py:51
  48.7 6.5 all-to-all-start
  55.2 0.0 reduce-scatter.3.cloned.1.call-start
  55.4 0.6 reduce_window_sum.11
  55.9 0.2 slice_reduce_fusion
  56.1 0.1 copy.25
  56.2 0.6 dynamic-slice
  57.4 0.1 convert_bitcast_fusion
  57.5 271.6 %all-to-all-done = bf16[2,128,24576]{1,0,2:T(2,128)(2,1)} async-done(((bf16[2,128,24576]{1,0,2:T(2,128)(2,1)}), bf16[2,128,24576]{1,0,2:T(2,128)(2,1)}, u32[]{:S(2)}, u32[]{:S(2)}) %all-to-all-start) | async-done | bytes 12582944 | tf_op jit(solution)/shard_map/all_to_all | solution.py:52
  329.1 31.3 %copy.36 = bf16[2,128,8,3072]{3,1,0,2:T(8,128)(2,1)} copy(bf16[2,128,8,3072]{1,0,3,2:T(2,128)(2,1)} %bitcast.2) | data formatting | bytes 25165824 | tf_op jit(solution)/shard_map/all_to_all | solution.py:52
  360.3 31.2 %copy.24 = bf16[2,128,8,3072]{3,1,2,0:T(8,128)(2,1)} copy(bf16[2,128,8,3072]{1,0,3,2:T(2,128)(2,1)} %bitcast.2) | data formatting | bytes 25165824 | tf_op jit(solution)/shard_map/all_to_all | solution.py:52
  391.5 6.3 fusion.6
  397.8 6.3 fusion.4
  404.2 6.3 fusion.8
  410.5 0.2 bitcast_add_fusion.2
  410.7 1.5 while.33
  410.8 0.1 bitcast_add_fusion.5
  411.0 0.1 bitcast_add_fusion.5
  411.2 0.1 bitcast_add_fusion.5
  411.4 0.1 bitcast_add_fusion.5
  411.5 0.1 bitcast_add_fusion.5
  411.7 0.1 bitcast_add_fusion.5
  411.9 0.1 bitcast_add_fusion.5
  412.1 0.1 bitcast_add_fusion.5
  412.2 0.4 dynamic-update-slice
  412.6 16.4 %fusion.12 = f32[2,8,128,3072]{3,2,1,0:T(8,128)} fusion(bf16[2,128,8,3072]{3,1,2,0:T(8,128)(2,1)} %copy.24, f32[2,8,128]{2,1,0:T(8,128)S(1)} %get-tuple-element.277, f32[2,8,128]{2,1,0:T(8,128)S(1)} %reduce_window_sum.11, f32[2,8,128]{2,1,0:T(8,128)S(1)} %get-tuple-element.274, pred[128,128]{1,0:T(8,128)(4,1)S(1)} %iota_compare_fusion), kind=kOutput, calls=%fused_computation.23 | convolution fusion | flops 1612709888 | bytes 37789696 | tf_op jit(solution)/shard_map/fbij,fbjp->fbip/dot_general | solution.py:73
  429.0 16.4 %fusion.10 = f32[2,8,128,3072]{3,2,1,0:T(8,128)} fusion(bf16[2,128,8,3072]{3,1,2,0:T(8,128)(2,1)} %copy.24, f32[2,8,128]{2,1,0:T(8,128)S(1)} %get-tuple-element.277, f32[2,8,128]{2,1,0:T(8,128)S(1)} %reduce_window_sum.11, f32[2,8,128]{2,1,0:T(8,128)S(1)} %get-tuple-element.274, pred[128,128]{1,0:T(8,128)(4,1)S(1)} %iota_compare_fusion), kind=kOutput, calls=%fused_computation.21 | convolution fusion | flops 1613496320 | bytes 37789696 | tf_op jit(solution)/shard_map/fbij,fbjp->fbip/dot_general | solution.py:73
  445.4 10.3 %all-reduce = f32[8]{0:T(128)S(1)} all-reduce(f32[8]{0:T(128)S(1)} %dynamic-update-slice), channel_id=2, replica_groups=mesh['tm'=4,'grid'=8] {'tm'}, use_global_device_ids=true, to_apply=%add | all-reduce | flops 8 | bytes 64
  455.6 0.1 reshape.48
  455.7 7.4 %all-gather.2 = f32[4,2,3072]{2,1,0:T(2,128)S(1)} all-gather(f32[1,2,3072]{2,1,0:T(2,128)S(1)} %bitcast.110), channel_id=3, replica_groups=mesh['tm'=4,'grid'=8] {'tm'}, dimensions={0}, use_global_device_ids=true | all-gather | bytes 122880 | tf_op jit(solution)/shard_map/all_gather | solution.py:11
  463.1 0.6 while.34
  463.3 0.1 fusion.55
  463.4 0.1 fusion.55
  463.6 0.1 fusion.55
  463.7 0.1 multiply_add_fusion
  463.8 0.1 add_bitcast_fusion
  463.9 0.1 copy.26
  464.0 30.7 %subtract_convert_fusion = bf16[2,8,128,3072]{3,2,1,0:T(8,128)(2,1)} fusion(f32[2,8,128,3072]{3,2,1,0:T(8,128)} %fusion.10, f32[2,8,128,3072]{3,2,1,0:T(8,128)} %fusion.12, bf16[2,128,8,3072]{3,1,2,0:T(8,128)(2,1)} %copy.24, f32[2,8,3072]{2,1,0:T(8,128)S(1)} %copy.26, f32[2,8,128]{2,1,0:T(8,128)S(1)} %get-tuple-element.273, ...), kind=kOutput, calls=%fused_computation.13 | convolution fusion | flops 1655963648 | bytes 75743232 | tf_op jit(solution)/shard_map/fbij,fbjp->fbip/dot_general | solution.py:73
  494.7 5.7 fusion.45
  500.4 1.8 convolution_bitcast_fusion.2
  502.2 0.8 copy-done.1
  503.1 1.8 convolution_bitcast_fusion.3
  504.9 0.1 copy-done.3
  504.9 1.5 pad_maximum_fusion.2
  506.4 0.0 reduce-scatter.3.cloned.1.call-update
  506.4 0.0 all-gather.5.cloned.1.call-start
  506.5 33.8 %reduce-scatter.3.cloned.1.call-done = f32[2,128,256]{2,1,0:T(8,128)} async-done(((f32[2,1024,256]{2,1,0:T(8,128)}), f32[2,128,256]{2,1,0:T(8,128)}) %reduce-scatter.3.cloned.1.call-update) | async-done | bytes 262160 | tf_op jit(solution)/shard_map/reduce_scatter | solution.py:115
  540.3 1.6 convert_element_type.51
  541.9 0.0 all-gather.5.cloned.1.call-update
  541.9 0.0 all-reduce.3.cloned.1.call-start
  542.0 21.3 %all-gather.5.cloned.1.call-done = bf16[2,1024,256]{2,1,0:T(8,128)(2,1)} async-done(((bf16[2,128,256]{2,1,0:T(8,128)(2,1)}), bf16[2,1024,256]{2,1,0:T(8,128)(2,1)}) %all-gather.5.cloned.1.call-update) | async-done | bytes 1048592 | tf_op jit(solution)/shard_map/all_gather | solution.py:118
  563.3 2.3 fusion.27
  565.6 0.0 all-reduce.3.cloned.1.call-update
  565.6 0.0 reduce-scatter.5.cloned.1.call-start
  565.7 5.0 convolution_bitcast_fusion
  570.7 1.8 convolution_bitcast_fusion.1
  572.5 3.1 pad_maximum_fusion.1
  575.6 0.0 reduce-scatter.5.cloned.1.call-update
  575.6 33.8 %all-reduce.3.cloned.1.call-done = f32[256,256]{1,0:T(8,128)} async-done(((f32[256,256]{1,0:T(8,128)}), f32[256,256]{1,0:T(8,128)}) %all-reduce.3.cloned.1.call-update) | async-done | bytes 262160 | tf_op jit(solution)/shard_map/psum | solution.py:130
  609.4 1.7 broadcast_multiply_fusion
  611.1 71.7 %reduce-scatter.5.cloned.1.call-done = f32[64,2,3072]{2,0,1:T(8,128)} async-done(((f32[256,2,3072]{2,0,1:T(8,128)}), f32[64,2,3072]{2,0,1:T(8,128)}) %reduce-scatter.5.cloned.1.call-update) | async-done | bytes 1572880 | tf_op jit(solution)/shard_map/reduce_scatter | solution.py:124
  682.7 2.7 fusion.18
  (54 shorter events, 0.7 us)
Async XLA Ops:
  7.2 493.3 %copy-start = (bf16[3072,256]{1,0:T(8,128)(2,1)S(1)}, bf16[3072,256]{1,0:T(8,128)(2,1)}, u32[]{:S(2)}) copy-start(bf16[3072,256]{1,0:T(8,128)(2,1)} %param.15) | copy-start | bytes 4718596
  48.7 6.6 copy-start.6
  48.7 7.5 %copy-start.8 = (u32[32]{0:T(128)S(1)}, u32[32]{0:T(128)}, u32[]{:S(2)}) copy-start(u32[32]{0:T(128)} %constant.59) | copy-start | bytes 388
  48.7 280.3 %all-to-all-start = ((bf16[2,128,24576]{1,0,2:T(2,128)(2,1)}), bf16[2,128,24576]{1,0,2:T(2,128)(2,1)}, u32[]{:S(2)}, u32[]{:S(2)}) async-start(bf16[2,128,24576]{1,0,2:T(2,128)(2,1)} %copy.22), calls=%async_computation | async-start | bytes 25165824 | tf_op jit(solution)/shard_map/all_to_all | solution.py:52
  55.2 485.1 %reduce-scatter.3.cloned.1.call-start = ((), (), s32[]{:S(2)}) async-start(), calls=%async_computation.3 | async-start | bytes 2359296 | tf_op jit(solution)/shard_map/reduce_scatter | solution.py:115
  429.0 34.7 %copy-start.5 = (f32[2,3072]{1,0:T(2,128)S(1)}, f32[2,3072]{1,0:T(2,128)}, u32[]{:S(2)}) copy-start(f32[2,3072]{1,0:T(2,128)} %param.13) | copy-start | bytes 73732
  494.6 8.4 %copy-start.7 = (bf16[3072,256]{1,0:T(8,128)(2,1)S(1)}, bf16[3072,256]{1,0:T(8,128)(2,1)}, u32[]{:S(2)}) copy-start(bf16[3072,256]{1,0:T(8,128)(2,1)} %param.14) | copy-start | bytes 4718596
  500.4 2.7 copy-start.1
  500.4 4.5 copy-start.3
  506.4 56.9 %all-gather.5.cloned.1.call-start = ((), (), s32[]{:S(2)}) async-start(), calls=%async_computation.4 | async-start | bytes 1179648 | tf_op jit(solution)/shard_map/all_gather | solution.py:118
  541.9 67.5 %all-reduce.3.cloned.1.call-start = ((), (), s32[]{:S(2)}) async-start(), calls=%async_computation.6 | async-start | bytes 524288 | tf_op jit(solution)/shard_map/psum | solution.py:130
  563.3 7.4 %copy-start.4 = (bf16[2,1024,256]{2,1,0:T(8,128)(2,1)S(1)}, bf16[2,1024,256]{2,1,0:T(8,128)(2,1)}, u32[]{:S(2)}) copy-start(bf16[2,1024,256]{2,1,0:T(8,128)(2,1)} %all-gather.5.cloned.1.call-done) | copy-start | bytes 3145732
  565.6 117.1 %reduce-scatter.5.cloned.1.call-start = ((), (), s32[]{:S(2)}) async-start(), calls=%async_computation.5 | async-start | bytes 7864320 | tf_op jit(solution)/shard_map/reduce_scatter | solution.py:124
  565.7 5.0 copy-start.2
Sparse Core Ops, SparseCore 0:
  506.5 33.6 reduce-scatter.2
  542.5 20.7 all-gather.4
  566.8 42.5 all-reduce.2
  612.5 70.1 reduce-scatter.4
where the time goes:
time: 695 us; the launch traced here: 692 us
  waiting for transfers between devices  432 us (62%)
  local copies, waits for them, and re-layouts  102 us (15%)
  matrix products  95.1 us (14%)
  other arithmetic  23.5 us (3%)
  blocking collectives  17.6 us (3%)
  between operations  14.6 us (2%)
    all_to_all x1, waiting for transfers between devices, per_device(): lax.all_to_all(piled_quantities, 'grid', split_axis=2, concat_axis=1, til...  272 us
    reduce_scatter x1, waiting for transfers between devices, per_device(): lax.psum_scatter(jnp.stack([onto_warmth, onto_wetness], axis=1), 'tm', sc...  71.7 us
    dot_general x3, matrix products, per_device(): jnp.einsum('fbij,fbjp->fbip', within_part, field_blocks, preferred_elemen...  63.4 us
    all_to_all x2, local copies, waits for them, and re-layouts, per_device(): lax.all_to_all(piled_quantities, 'grid', split_axis=2, concat_axis=1, til...  62.5 us
    reduce_scatter x1, waiting for transfers between devices, per_device(): lax.psum_scatter(partials, 'grid', scatter_dimension=1, tiled=True)  33.8 us
    psum x1, waiting for transfers between devices, per_device(): kernel_middle = lax.psum(cross_part, 'tm') * divisor_magnitude  33.8 us
    another operation x1, local copies, waits for them, and re-layouts, per_device(): piled_quantities = jnp.stack([clocked_seawarmth, clocked_precipitation])  31 us
    all_gather x1, waiting for transfers between devices, per_device(): compressed_lines = lax.all_gather(shares, 'grid', axis=1, tiled=True)  21.3 us
  transfers between devices with their start and end apart: 5, of which 5 were waited for; matrix products, arithmetic and copies ran while one was open for 2% of the time, Pallas kernels for 0%

commit v1 on v0

v1 whole, which is shorter than its diff:
```python
import functools

import jax
import jax.numpy as jnp
from jax import lax
from jax.experimental import pallas as pl
from jax.experimental.pallas import tpu as pltpu
from jax.sharding import Mesh, PartitionSpec as P

MESH = pl.DeviceIdType.MESH
VMEM_LIMIT = 56 * 1024 * 1024


def flip(index, mask, count):
    out, bit = 0, 1
    while bit < count:
        out = out + lax.rem(lax.div(index, bit) + (mask // bit) % 2, 2) * bit
        bit *= 2
    return out


def greet(count, where):
    barrier = pltpu.get_barrier_semaphore()
    for mask in range(1, count):
        pl.semaphore_signal(barrier, inc=1, device_id=where(mask), device_id_type=MESH)
    pl.semaphore_wait(barrier, count - 1)


def group_peer(mask, nb):
    mine = lax.axis_index("tm") * 2 + lax.axis_index("cc")
    peer = flip(mine, mask, nb)
    return peer, (lax.div(peer, 2), lax.axis_index("zz"), lax.rem(peer, 2))


def exchange_kernel(nt, nz, sub, warm, wet, out, send_sem, recv_sem, own_sem):
    nb = nt * 2
    mine = lax.axis_index("tm") * 2 + lax.axis_index("cc")
    greet(nb, lambda mask: group_peer(mask, nb)[1])

    def columns(block, z):
        start = (z * 2 + lax.rem(block, 2)) * (nt * sub) + lax.div(block, 2) * sub
        return pl.ds(pl.multiple_of(start, 128), sub)

    order = list(range(nb - 1, 0, -1))
    for f, source in enumerate((warm, wet)):
        for z in range(nz):
            for mask in order:
                peer, device = group_peer(mask, nb)
                pltpu.make_async_remote_copy(
                    src_ref=source.at[:, columns(peer, z)],
                    dst_ref=out.at[f, mine, :, pl.ds(z * sub, sub)],
                    send_sem=send_sem.at[f, mask - 1],
                    recv_sem=recv_sem.at[f, mask - 1],
                    device_id=device,
                    device_id_type=MESH,
                ).start()
            pltpu.make_async_copy(
                source.at[:, columns(mine, z)],
                out.at[f, mine, :, pl.ds(z * sub, sub)],
                own_sem.at[f],
            ).start()
    for f in range(2):
        pltpu.make_async_copy(out.at[f, mine], out.at[f, mine], own_sem.at[f]).wait()
        for mask in order:
            peer, device = group_peer(mask, nb)
            whole = pltpu.make_async_remote_copy(
                src_ref=out.at[f, peer],
                dst_ref=out.at[f, peer],
                send_sem=send_sem.at[f, mask - 1],
                recv_sem=recv_sem.at[f, mask - 1],
                device_id=device,
                device_id_type=MESH,
            )
            whole.wait_send()
            whole.wait_recv()


def exchange(warm, wet, nt, nz, sub):
    nb = nt * 2
    hours = warm.shape[0]
    return pl.pallas_call(
        functools.partial(exchange_kernel, nt, nz, sub),
        out_shape=jax.ShapeDtypeStruct((2, nb, hours, nz * sub), jnp.bfloat16),
        in_specs=[pl.BlockSpec(memory_space=pl.ANY)] * 2,
        out_specs=pl.BlockSpec(memory_space=pl.ANY),
        scratch_shapes=[
            pltpu.SemaphoreType.DMA((2, nb - 1)),
            pltpu.SemaphoreType.DMA((2, nb - 1)),
            pltpu.SemaphoreType.DMA((2,)),
        ],
        compiler_params=pltpu.CompilerParams(collective_id=0, has_side_effects=True),
        cost_estimate=pl.CostEstimate(flops=10**11, bytes_accessed=10**8, transcendentals=0),
        name="exchange",
    )(warm, wet)


def ends_kernel(weights, x, ends):
    for f in range(2):
        for b in range(x.shape[1]):
            rows = jnp.dot(weights[f, b], x[f, b], preferred_element_type=jnp.float32)
            ends[f, b : b + 1, :] = jnp.sum(rows, axis=0, keepdims=True)


def block_ends(weights, x, sub):
    _, nb, hours, width = x.shape
    return pl.pallas_call(
        ends_kernel,
        grid=(width // sub,),
        out_shape=jax.ShapeDtypeStruct((2, nb, width), jnp.float32),
        in_specs=[
            pl.BlockSpec(weights.shape, lambda i: (0, 0, 0, 0)),
            pl.BlockSpec((2, nb, hours, sub), lambda i: (0, 0, 0, i)),
        ],
        out_specs=pl.BlockSpec((2, nb, sub), lambda i: (0, 0, i)),
        compiler_params=pltpu.CompilerParams(vmem_limit_bytes=VMEM_LIMIT),
        name="block_ends",
    )(weights, x)


def anomaly_kernel(nt, nz, gains, within, fade, ends, start, x, operator, anomaly, proj):
    nb = nt * 2
    z_mine = lax.axis_index("zz")

    @pl.when(pl.program_id(0) == 0)
    def _():
        proj[...] = jnp.zeros_like(proj)

    for f in range(2):
        level = start[0, f : f + 1, :]
        entering = [level] * nb
        for t in range(nt):
            for z in range(nz):
                for c in range(2):
                    b = t * 2 + c
                    entering[b] = jnp.where(z_mine == z, level, entering[b])
                    step = (t * nz + z) * 2 + c
                    level = gains[f, step] * level + ends[z, f, b : b + 1, :]
        for b in range(nb):
            values = x[f, b]
            twice = jnp.concatenate([values, values], axis=0)
            inside = jnp.dot(within[f, b], twice, preferred_element_type=jnp.float32)
            previous = inside + fade[f, b] * entering[b]
            departure = (values.astype(jnp.float32) - previous).astype(jnp.bfloat16)
            anomaly[f, b] = departure
            proj[f, b] += jnp.dot(departure, operator[f], preferred_element_type=jnp.float32)


def anomalies(gains, within, fade, ends, start, x, operator, nt, nz, sub):
    _, nb, hours, width = x.shape
    rank = operator.shape[-1]
    return pl.pallas_call(
        functools.partial(anomaly_kernel, nt, nz),
        grid=(nz,),
        out_shape=(
            jax.ShapeDtypeStruct(x.shape, jnp.bfloat16),
            jax.ShapeDtypeStruct((2, nb, hours, rank), jnp.float32),
        ),
        in_specs=[
            pl.BlockSpec(memory_space=pltpu.SMEM),
            pl.BlockSpec(within.shape, lambda i: (0, 0, 0, 0)),
            pl.BlockSpec(fade.shape, lambda i: (0, 0, 0, 0)),
            pl.BlockSpec((nz, 2, nb, sub), lambda i: (0, 0, 0, i)),
            pl.BlockSpec((1, 2, sub), lambda i: (i, 0, 0)),
            pl.BlockSpec((2, nb, hours, sub), lambda i: (0, 0, 0, i)),
            pl.BlockSpec((2, sub, rank), lambda i: (0, i, 0)),
        ],
        out_specs=(
            pl.BlockSpec((2, nb, hours, sub), lambda i: (0, 0, 0, i)),
            pl.BlockSpec((2, nb, hours, rank), lambda i: (0, 0, 0, 0)),
        ),
        compiler_params=pltpu.CompilerParams(vmem_limit_bytes=VMEM_LIMIT),
        name="anomalies",
    )(gains, within, fade, ends, start, x, operator)


def split(weights, count):
    parts = []
    for _ in range(count):
        part = weights.astype(jnp.bfloat16)
        parts.append(part)
        weights = weights - part.astype(jnp.float32)
    return parts


def over_hours(left, right):
    return lax.dot_general(
        left, right, (((0,), (0,)), ((), ())), preferred_element_type=jnp.float32
    )


def per_device(warm, wet, fading, starting, warmth_operator, wetness_operator):
    nt, nz = lax.axis_size("tm"), lax.axis_size("zz")
    t_mine, z_mine = lax.axis_index("tm"), lax.axis_index("zz")
    nb = nt * 2
    hours = warm.shape[0]
    sub = warm.shape[1] // (nb * nz)
    rank = warmth_operator.shape[1]

    operator = lax.dynamic_slice_in_dim(
        jnp.stack([warmth_operator, wetness_operator]), t_mine * sub, sub, axis=1
    )
    operator = lax.all_gather(operator, "zz", axis=1, tiled=True)
    start = lax.all_gather(lax.dynamic_slice_in_dim(starting, t_mine * sub, sub, axis=1), "zz")
    fading = lax.all_gather(fading, "tm", axis=1, tiled=True)

    x = exchange(warm, wet, nt, nz, sub)

    every = fading.reshape(2, nt, nz, 2, hours)
    gains = jnp.exp(jnp.sum(jnp.log(every), axis=-1)).reshape(2, nt * nz * 2)
    decay = lax.dynamic_index_in_dim(every, z_mine, 2, keepdims=False).reshape(2, nb, hours)
    log_decay = jnp.log(decay)
    row = lax.broadcasted_iota(jnp.int32, (hours, hours), 0)
    col = lax.broadcasted_iota(jnp.int32, (hours, hours), 1)
    inclusive = jnp.sum(jnp.where(row >= col, log_decay[:, :, None, :], 0.0), axis=-1)
    exclusive = inclusive - log_decay
    spread = exclusive[..., :, None] - inclusive[..., None, :]
    within = (
        jnp.where(row > col, jnp.exp(jnp.minimum(spread, 0.0)), 0.0)
        * (1.0 - decay)[..., None, :]
    )
    within = jnp.concatenate(split(within, 2), axis=-1)
    to_end = jnp.exp(inclusive[..., -1:] - inclusive) * (1.0 - decay)
    to_end = jnp.stack(split(to_end, 3), axis=2)
    to_end = jnp.pad(to_end, ((0, 0), (0, 0), (0, 13), (0, 0)))
    fade = jnp.exp(exclusive)[..., None]

    ends = lax.all_gather(block_ends(to_end, x, sub), "zz")
    anomaly, proj = anomalies(gains, within, fade, ends, start, x, operator, nt, nz, sub)
    share = lax.psum_scatter(
        proj.reshape(2, nb * hours, rank), ("tm", "cc"), scatter_dimension=1, tiled=True
    ).astype(jnp.bfloat16)
    lines = lax.all_gather(share, ("tm", "cc"), axis=1, tiled=True)
    anomaly = anomaly.reshape(2, nb * hours, nz * sub)
    scale = (nb * nz * hours) ** (-0.5)
    sketches = jnp.stack(
        [over_hours(lines[1], anomaly[0]), over_hours(lines[0], anomaly[1])]
    ).astype(jnp.bfloat16)
    middle = lax.psum(over_hours(lines[0], lines[1]), "zz") * scale
    sums = lax.psum_scatter(sketches, "zz", scatter_dimension=2, tiled=True)
    sums = lax.all_to_all(sums, "tm", split_axis=1, concat_axis=2, tiled=True)
    sums = sums.astype(jnp.float32) * scale
    return sums[0], sums[1], middle


def solution(mesh):
    nt, ng = mesh.devices.shape
    mesh = Mesh(mesh.devices.reshape(nt, ng // 2, 2), ("tm", "zz", "cc"))
    grid = ("zz", "cc")
    return jax.shard_map(
        per_device,
        mesh=mesh,
        in_specs=(
            P(("tm", "zz", "cc"), None),
            P(("tm", "zz", "cc"), None),
            P(None, "tm"),
            P(None, grid),
            P(grid, None),
            P(grid, None),
        ),
        out_specs=(P("tm", grid), P("tm", grid), P()),
        check_vma=False,
    )
```

time: 695 us -> 415 us (0.60)
  waiting for transfers between devices: 432 us -> 153 us
  Pallas kernels: 0 us -> 164 us
  matrix products: 95.1 us -> 7.84 us
  local copies, waits for them, and re-layouts: 102 us -> 20.4 us
  blocking collectives: 17.6 us -> 40.5 us
  other arithmetic: 23.5 us -> 10.8 us
    all_to_all x1, waiting for transfers between devices: 272 us -> 0.01 us  [per_device(): sums = lax.all_to_all(sums, 'tm', split_axis=1, concat_axis=2, tiled=True)]
    pallas_call x0 -> x3, Pallas kernels: none -> 164 us  [the longest x1 141 us: exchange(): pl.pallas_call(functools.partial(exchange_kernel, nt, nz, sub), out_shape...]
    dot_general x11 -> x3, matrix products: 95.1 us -> 7.84 us  [over_hours(): lax.dot_general(left, right, (((0,), (0,)), ((), ())), preferred_element_...]
    all_to_all x2 -> x0, local copies, waits for them, and re-layouts: 62.5 us -> none  [per_device(): lax.all_to_all(piled_quantities, 'grid', split_axis=2, concat_axis=1, til...]
    all_gather x1 -> x3, blocking collectives: 7.38 us -> 40.5 us  [the longest x1 18.2 us: per_device(): ends = lax.all_gather(block_ends(to_end, x, sub), 'zz')]
    another operation x1 -> x0, local copies, waits for them, and re-layouts: 31 us -> none  [per_device(): piled_quantities = jnp.stack([clocked_seawarmth, clocked_precipitation])]
    another operation x5 -> x3, other arithmetic: 15.7 us -> 4.62 us  [the longest x1 2.05 us: per_device(): jnp.stack([warmth_operator, wetness_operator])]
    unnamed x1 -> x0, blocking collectives: 10.3 us -> none
  transfers between devices with their start and end apart: 5 -> 6, of which waited for: 5 -> 4; matrix products, arithmetic and copies ran while one was open for 2% -> 5% of each run, Pallas kernels for 0% -> 36%
where the time goes in v1:
time: 415 us
  Pallas kernels  164 us (40%)
  waiting for transfers between devices  153 us (37%)
  blocking collectives  40.5 us (10%)
  local copies, waits for them, and re-layouts  20.4 us (5%)
  between operations  14 us (3%)
  other arithmetic  10.8 us (3%)
  matrix products  7.84 us (2%)
    pallas_call x1, Pallas kernels, exchange(): pl.pallas_call(functools.partial(exchange_kernel, nt, nz, sub), out_shape...  141 us
    reduce_scatter x1, waiting for transfers between devices, per_device(): sums = lax.psum_scatter(sketches, 'zz', scatter_dimension=2, tiled=True)  60.4 us
    reduce_scatter x1, waiting for transfers between devices, per_device(): lax.psum_scatter(proj.reshape(2, nb * hours, rank), ('tm', 'cc'), scatter...  40.9 us
    psum x1, waiting for transfers between devices, per_device(): middle = lax.psum(over_hours(lines[0], lines[1]), 'zz') * scale  38.3 us
    all_gather x1, blocking collectives, per_device(): ends = lax.all_gather(block_ends(to_end, x, sub), 'zz')  18.2 us
    pallas_call x1, Pallas kernels, anomalies(): pl.pallas_call(functools.partial(anomaly_kernel, nt, nz), grid=(nz,), out...  16 us
    all_gather x1, blocking collectives, per_device(): lax.all_gather(lax.dynamic_slice_in_dim(starting, t_mine * sub, sub, axis...  14.1 us
    all_gather x1, waiting for transfers between devices, per_device(): lines = lax.all_gather(share, ('tm', 'cc'), axis=1, tiled=True)  13.6 us
  transfers between devices with their start and end apart: 6, of which 4 were waited for; matrix products, arithmetic and copies ran while one was open for 5% of the time, Pallas kernels for 36%

profile of v1, /device:TPU:0, one launch (start us, length us, event | category | flops | bytes accessed | tf_op | source)
XLA Modules:
  0.0 414.7 jit_solution(7363193532917409850)
XLA Ops:
  7.2 0.0 copy-start
  7.2 0.0 all-gather.6.cloned.1.call-start
  7.2 2.0 fusion.3
  9.3 0.0 all-gather.6.cloned.1.call-update
  9.3 0.0 copy-start.4
  9.3 0.0 reduce-scatter.3.cloned.1.call-start
  9.4 141.3 %exchange.1.x = bf16[2,8,128,3072]{3,2,1,0:T(8,128)(2,1)} custom-call(bf16[128,24576]{1,0:T(8,128)(2,1)} %warm.1, bf16[128,24576]{1,0:T(8,128)(2,1)} %wet.1), custom_call_target="tpu_custom_call" | custom-call | flops 99999997952 | bytes 100000000 | tf_op jit(solution)/shard_map/exchange/pallas_call | solution.py:81
  150.7 0.0 copy-done.4
  150.7 8.2 %all_gather.21 = f32[2,4096]{1,0:T(2,128)S(1)} all-gather(f32[2,1024]{1,0:T(2,128)S(1)} %copy-done.4), channel_id=1, replica_groups=mesh['tm'=4,'zz'=4,'cc'=2] {'tm'}, dimensions={1}, use_global_device_ids=true | all-gather | bytes 40960 | tf_op jit(solution)/shard_map/all_gather | solution.py:204
  158.9 0.1 log_reduce_fusion
  159.1 0.7 exp.39.gains
  159.8 0.3 select_reduce_fusion
  160.2 0.4 copy.27
  160.5 1.1 exp.41.fade
  161.7 0.2 slice_reduce_fusion
  161.8 0.1 fusion.10
  161.9 0.7 fusion.9.weights
  162.6 6.9 %block_ends.1 = f32[2,8,3072]{2,1,0:T(8,128)} custom-call(bf16[2,8,16,128]{3,2,1,0:T(8,128)(2,1)} %fusion.9.weights, bf16[2,8,128,3072]{3,2,1,0:T(8,128)(2,1)} %exchange.1.x), custom_call_target="tpu_custom_call" | custom-call | tf_op jit(solution)/shard_map/block_ends/pallas_call | solution.py:106
  169.5 0.0 copy-done
  169.5 0.0 copy-start.3
  169.5 14.1 %all-gather.2.start = f32[4,2,768]{2,1,0:T(2,128)} all-gather(f32[1,2,768]{2,1,0:T(2,128)S(1)} %dynamic-slice_bitcast_fusion), channel_id=3, replica_groups=mesh['tm'=4,'zz'=4,'cc'=2] {'zz'}, dimensions={0}, use_global_device_ids=true | all-gather | bytes 30720 | tf_op jit(solution)/shard_map/all_gather | solution.py:203
  183.6 0.4 fusion.2
  184.0 1.1 pad_maximum_fusion.1.within
  185.1 0.0 copy-done.3
  185.1 18.2 %all-gather = f32[8,8,3072]{2,1,0:T(8,128)} all-gather(f32[2,8,3072]{2,1,0:T(8,128)S(1)} %copy-done.3), channel_id=2, replica_groups=mesh['tm'=4,'zz'=4,'cc'=2] {'zz'}, dimensions={0}, use_global_device_ids=true | all-gather | bytes 983040 | tf_op jit(solution)/shard_map/all_gather | solution.py:227
  203.3 0.0 all-gather.6.cloned.1.call-done.operator
  203.3 16.0 %anomalies.1 = (bf16[2,8,128,3072]{3,2,1,0:T(8,128)(2,1)}, f32[2,8,128,256]{3,2,1,0:T(8,128)}) custom-call(f32[2,32]{1,0:T(2,128)} %exp.39.gains, bf16[2,8,128,256]{3,2,1,0:T(8,128)(2,1)} %pad_maximum_fusion.1.within, f32[2,8,128,1]{3,2,1,0:T(8,128)} %exp.41.fade, f32[4,2,8,3072]{3,2,1,0:T(8,128)} %bitcast.52, f32[4,2,768]{2,1,0:T(2,128)} %all-gather.2.start, ...), custom_call_target="tpu_custom_call" | custom-call | tf_op jit(solution)/shard_map/anomalies/pallas_call | solution.py:151
  219.3 0.0 reduce-scatter.3.cloned.1.call-update
  219.3 0.0 all-gather.8.cloned.1.call-start
  219.4 40.9 %reduce-scatter.3.cloned.1.call-done = f32[2,128,256]{2,1,0:T(8,128)} async-done(((f32[2,1024,256]{2,1,0:T(8,128)}), f32[2,128,256]{2,1,0:T(8,128)}) %reduce-scatter.3.cloned.1.call-update) | async-done | bytes 262160 | tf_op jit(solution)/shard_map/reduce_scatter | solution.py:229
  260.2 1.6 convert_element_type.95
  261.9 0.0 all-gather.8.cloned.1.call-update
  261.9 0.0 reduce-scatter.5.cloned.1.call-start
  261.9 10.8 %fusion.12 = (bf16[1,8,128,3072]{3,2,1,0:T(8,128)(2,1)}, bf16[1,8,128,3072]{3,2,1,0:T(8,128)(2,1)}) fusion(bf16[2,8,128,3072]{3,2,1,0:T(8,128)(2,1)} %get-tuple-element.6), kind=kLoop, calls=%fused_computation.38 | loop fusion | bytes 25165824 | tf_op jit(solution)/shard_map/slice | solution.py:236
  272.8 13.6 %all-gather.8.cloned.1.call-done = bf16[2,1024,256]{2,1,0:T(8,128)(2,1)} async-done(((bf16[2,128,256]{2,1,0:T(8,128)(2,1)}), bf16[2,1024,256]{2,1,0:T(8,128)(2,1)}) %all-gather.8.cloned.1.call-update) | async-done | bytes 1048592 | tf_op jit(solution)/shard_map/all_gather | solution.py:232
  286.4 0.0 copy-start.1
  286.4 0.0 copy-start.2
  286.4 4.9 %fusion = bf16[1,256,3072]{2,1,0:T(8,128)(2,1)S(1)} fusion(bf16[1024,3072]{1,0:T(8,128)(2,1)} %bitcast.50, bf16[2,1024,256]{2,1,0:T(8,128)(2,1)} %all-gather.8.cloned.1.call-done), kind=kOutput, calls=%fused_computation.2 | convolution fusion | flops 1611399168 | bytes 8388608 | tf_op jit(solution)/shard_map/dot_general | solution.py:186
  291.3 0.0 copy-done.1
  291.3 0.0 copy-done.2
  291.4 1.9 fusion.1
  293.3 1.9 pad_maximum_fusion
  295.2 0.0 reduce-scatter.5.cloned.1.call-update
  295.2 60.4 %reduce-scatter.5.cloned.1.call-done = bf16[2,256,768]{2,1,0:T(8,128)(2,1)} async-done(((bf16[2,256,3072]{2,1,0:T(8,128)(2,1)}), bf16[2,256,768]{2,1,0:T(8,128)(2,1)}) %reduce-scatter.5.cloned.1.call-update) | async-done | bytes 786448 | tf_op jit(solution)/shard_map/reduce_scatter | solution.py:239
  355.6 2.8 copy.29
  358.4 3.7 all-to-all-start
  362.1 0.1 all-reduce.3.cloned.1.call-start
  362.2 1.0 fusion.4
  363.2 0.0 all-reduce.3.cloned.1.call-update
  363.2 38.3 %all-reduce.3.cloned.1.call-done = f32[256,256]{1,0:T(8,128)} async-done(((f32[256,256]{1,0:T(8,128)}), f32[256,256]{1,0:T(8,128)}) %all-reduce.3.cloned.1.call-update) | async-done | bytes 262160 | tf_op jit(solution)/shard_map/psum | solution.py:238
  401.5 1.7 broadcast_multiply_fusion
  403.2 0.0 all-to-all-done
  403.2 0.7 convert_multiply_fusion
  403.9 1.2 fusion.13
  405.1 0.5 copy.31
  405.6 1.0 copy.34
  406.7 0.5 copy.30
  407.2 1.0 copy.33
  (9 shorter events, 0.1 us)
Async XLA Ops:
  7.2 162.3 %copy-start = (f32[2,3072]{1,0:T(2,128)S(1)}, f32[2,3072]{1,0:T(2,128)}, u32[]{:S(2)}) copy-start(f32[2,3072]{1,0:T(2,128)} %param.9) | copy-start | bytes 73732
  7.2 196.2 %all-gather.6.cloned.1.call-start = ((), (), s32[]{:S(2)}) async-start(), calls=%async_computation.3 | async-start | bytes 3932160 | tf_op jit(solution)/shard_map/all_gather | solution.py:202
  9.3 141.4 %copy-start.4 = (f32[2,1024]{1,0:T(2,128)S(1)}, f32[2,1024]{1,0:T(2,128)}, u32[]{:S(2)}) copy-start(f32[2,1024]{1,0:T(2,128)} %param.8) | copy-start | bytes 24580
  9.3 250.9 %reduce-scatter.3.cloned.1.call-start = ((), (), s32[]{:S(2)}) async-start(), calls=%async_computation.4 | async-start | bytes 2359296 | tf_op jit(solution)/shard_map/reduce_scatter | solution.py:229
  169.5 15.6 %copy-start.3 = (f32[2,8,3072]{2,1,0:T(8,128)S(1)}, f32[2,8,3072]{2,1,0:T(8,128)}, u32[]{:S(2)}) copy-start(f32[2,8,3072]{2,1,0:T(8,128)} %block_ends.1) | copy-start | bytes 589828
  219.3 67.1 %all-gather.8.cloned.1.call-start = ((), (), s32[]{:S(2)}) async-start(), calls=%async_computation.5 | async-start | bytes 1179648 | tf_op jit(solution)/shard_map/all_gather | solution.py:232
  261.9 93.7 %reduce-scatter.5.cloned.1.call-start = ((), (), s32[]{:S(2)}) async-start(), calls=%async_computation.6 | async-start | bytes 3932160 | tf_op jit(solution)/shard_map/reduce_scatter | solution.py:239
  286.4 4.9 %copy-start.1 = (bf16[1,8,128,3072]{3,2,1,0:T(8,128)(2,1)S(1)}, bf16[1,8,128,3072]{3,2,1,0:T(8,128)(2,1)}, u32[]{:S(2)}) copy-start(bf16[1,8,128,3072]{3,2,1,0:T(8,128)(2,1)} %get-tuple-element.8) | copy-start | bytes 18874372
  286.4 5.0 %copy-start.2 = (bf16[2,1024,256]{2,1,0:T(8,128)(2,1)S(1)}, bf16[2,1024,256]{2,1,0:T(8,128)(2,1)}, u32[]{:S(2)}) copy-start(bf16[2,1024,256]{2,1,0:T(8,128)(2,1)} %all-gather.8.cloned.1.call-done) | copy-start | bytes 3145732
  358.4 44.8 %all-to-all-start = ((bf16[2,256,768]{2,0,1:T(2,128)(2,1)}), bf16[2,256,768]{2,0,1:T(2,128)(2,1)S(1)}, u32[]{:S(2)}, u32[]{:S(2)}) async-start(bf16[2,256,768]{2,0,1:T(2,128)(2,1)} %copy.29), calls=%async_computation.2 | async-start | bytes 1572864 | tf_op jit(solution)/shard_map/all_to_all | solution.py:240
  362.1 39.5 %all-reduce.3.cloned.1.call-start = ((), (), s32[]{:S(2)}) async-start(), calls=%async_computation.7 | async-start | bytes 524288 | tf_op jit(solution)/shard_map/psum | solution.py:238
Sparse Core Ops, SparseCore 0:
  10.2 66.1 all-gather.5
  219.4 40.7 reduce-scatter.2
  262.9 23.4 all-gather.7
  295.3 60.2 reduce-scatter.4
  365.6 35.8 all-reduce.2

commit v2 on v1

--- a/solution.py
+++ b/solution.py
@@ -32,7 +32,9 @@
     return peer, (lax.div(peer, 2), lax.axis_index("zz"), lax.rem(peer, 2))
 
 
-def exchange_kernel(nt, nz, sub, warm, wet, out, send_sem, recv_sem, own_sem):
+def exchange_kernel(
+    nt, nz, sub, warm, wet, fading, out, decays, send_sem, recv_sem, own_sem, fade_send, fade_recv
+):
     nb = nt * 2
     mine = lax.axis_index("tm") * 2 + lax.axis_index("cc")
     greet(nb, lambda mask: group_peer(mask, nb)[1])
@@ -42,6 +44,21 @@
         return pl.ds(pl.multiple_of(start, 128), sub)
 
     order = list(range(nb - 1, 0, -1))
+
+    def fade_copy(mask):
+        return pltpu.make_async_remote_copy(
+            src_ref=fading,
+            dst_ref=decays.at[mine],
+            send_sem=fade_send.at[mask - 1],
+            recv_sem=fade_recv.at[mask - 1],
+            device_id=group_peer(mask, nb)[1],
+            device_id_type=MESH,
+        )
+
+    for mask in order:
+        fade_copy(mask).start()
+    own_fade = pltpu.make_async_copy(fading, decays.at[mine], own_sem.at[2])
+    own_fade.start()
     for f, source in enumerate((warm, wet)):
         for z in range(nz):
             for mask in order:
@@ -73,25 +90,33 @@
             )
             whole.wait_send()
             whole.wait_recv()
-
-
-def exchange(warm, wet, nt, nz, sub):
+    own_fade.wait()
+    for mask in order:
+        fade_copy(mask).wait()
+
+
+def exchange(warm, wet, fading, nt, nz, sub):
     nb = nt * 2
     hours = warm.shape[0]
     return pl.pallas_call(
         functools.partial(exchange_kernel, nt, nz, sub),
-        out_shape=jax.ShapeDtypeStruct((2, nb, hours, nz * sub), jnp.bfloat16),
-        in_specs=[pl.BlockSpec(memory_space=pl.ANY)] * 2,
-        out_specs=pl.BlockSpec(memory_space=pl.ANY),
+        out_shape=(
+            jax.ShapeDtypeStruct((2, nb, hours, nz * sub), jnp.bfloat16),
+            jax.ShapeDtypeStruct((nb,) + fading.shape, jnp.float32),
+        ),
+        in_specs=[pl.BlockSpec(memory_space=pl.ANY)] * 3,
+        out_specs=(pl.BlockSpec(memory_space=pl.ANY),) * 2,
         scratch_shapes=[
             pltpu.SemaphoreType.DMA((2, nb - 1)),
             pltpu.SemaphoreType.DMA((2, nb - 1)),
-            pltpu.SemaphoreType.DMA((2,)),
+            pltpu.SemaphoreType.DMA((3,)),
+            pltpu.SemaphoreType.DMA((nb - 1,)),
+            pltpu.SemaphoreType.DMA((nb - 1,)),
         ],
         compiler_params=pltpu.CompilerParams(collective_id=0, has_side_effects=True),
         cost_estimate=pl.CostEstimate(flops=10**11, bytes_accessed=10**8, transcendentals=0),
         name="exchange",
-    )(warm, wet)
+    )(warm, wet, fading)
 
 
 def ends_kernel(weights, x, ends):
@@ -117,13 +142,13 @@
     )(weights, x)
 
 
-def anomaly_kernel(nt, nz, gains, within, fade, ends, start, x, operator, anomaly, proj):
+def anomaly_kernel(nt, nz, gains, within, fade, ends, start, x, operator, anomaly, proj, total):
     nb = nt * 2
     z_mine = lax.axis_index("zz")
 
     @pl.when(pl.program_id(0) == 0)
     def _():
-        proj[...] = jnp.zeros_like(proj)
+        total[...] = jnp.zeros_like(total)
 
     for f in range(2):
         level = start[0, f : f + 1, :]
@@ -142,7 +167,11 @@
             previous = inside + fade[f, b] * entering[b]
             departure = (values.astype(jnp.float32) - previous).astype(jnp.bfloat16)
             anomaly[f, b] = departure
-            proj[f, b] += jnp.dot(departure, operator[f], preferred_element_type=jnp.float32)
+            total[b, f] += jnp.dot(departure, operator[0, f], preferred_element_type=jnp.float32)
+
+    @pl.when(pl.program_id(0) == pl.num_programs(0) - 1)
+    def _():
+        proj[...] = total[...].astype(proj.dtype)
 
 
 def anomalies(gains, within, fade, ends, start, x, operator, nt, nz, sub):
@@ -153,7 +182,7 @@
         grid=(nz,),
         out_shape=(
             jax.ShapeDtypeStruct(x.shape, jnp.bfloat16),
-            jax.ShapeDtypeStruct((2, nb, hours, rank), jnp.float32),
+            jax.ShapeDtypeStruct((nb, 2, hours, rank), jnp.bfloat16),
         ),
         in_specs=[
             pl.BlockSpec(memory_space=pltpu.SMEM),
@@ -162,30 +191,171 @@
             pl.BlockSpec((nz, 2, nb, sub), lambda i: (0, 0, 0, i)),
             pl.BlockSpec((1, 2, sub), lambda i: (i, 0, 0)),
             pl.BlockSpec((2, nb, hours, sub), lambda i: (0, 0, 0, i)),
-            pl.BlockSpec((2, sub, rank), lambda i: (0, i, 0)),
+            pl.BlockSpec((1, 2, sub, rank), lambda i: (i, 0, 0, 0)),
         ],
         out_specs=(
             pl.BlockSpec((2, nb, hours, sub), lambda i: (0, 0, 0, i)),
-            pl.BlockSpec((2, nb, hours, rank), lambda i: (0, 0, 0, 0)),
-        ),
+            pl.BlockSpec((nb, 2, hours, rank), lambda i: (0, 0, 0, 0)),
+        ),
+        scratch_shapes=[pltpu.VMEM((nb, 2, hours, rank), jnp.float32)],
         compiler_params=pltpu.CompilerParams(vmem_limit_bytes=VMEM_LIMIT),
         name="anomalies",
     )(gains, within, fade, ends, start, x, operator)
-
-
-def split(weights, count):
-    parts = []
-    for _ in range(count):
-        part = weights.astype(jnp.bfloat16)
-        parts.append(part)
-        weights = weights - part.astype(jnp.float32)
-    return parts
 
 
 def over_hours(left, right):
     return lax.dot_general(
         left, right, (((0,), (0,)), ((), ())), preferred_element_type=jnp.float32
     )
+
+
+def sketch_kernel(
+    nt, nz, sub, proj, anomaly, sketch, middle,
+    held, parts, lines, cross, planes, rows,
+    load_sem, part_send, part_recv, line_send, line_recv,
+    plane_send, plane_recv, row_send, row_recv,
+):
+    nb = nt * 2
+    t, z, c = lax.axis_index("tm"), lax.axis_index("zz"), lax.axis_index("cc")
+    mine = t * 2 + c
+    hours, rank = proj.shape[2:]
+    share = rank // nb
+    masks = range(1, nb)
+    load = pltpu.make_async_copy(anomaly, held, load_sem)
+    load.start()
+
+    def z_peer(step):
+        return (t, lax.rem(z + step, nz), c)
+
+    barrier = pltpu.get_barrier_semaphore()
+    for mask in masks:
+        pl.semaphore_signal(barrier, inc=1, device_id=group_peer(mask, nb)[1], device_id_type=MESH)
+    for step in range(1, nz):
+        pl.semaphore_signal(barrier, inc=1, device_id=z_peer(step), device_id_type=MESH)
+    pl.semaphore_wait(barrier, nb - 1 + nz - 1)
+
+    def to_group(mask, src, dst, send, recv):
+        return pltpu.make_async_remote_copy(
+            src_ref=src,
+            dst_ref=dst,
+            send_sem=send.at[mask - 1],
+            recv_sem=recv.at[mask - 1],
+            device_id=group_peer(mask, nb)[1],
+            device_id_type=MESH,
+        )
+
+    copies = [
+        to_group(m, proj.at[group_peer(m, nb)[0]], parts.at[m - 1], part_send, part_recv)
+        for m in masks
+    ]
+    for copy in copies:
+        copy.start()
+    total = proj[mine].astype(jnp.float32)
+    for m, copy in zip(masks, copies):
+        copy.wait_recv()
+        total = total + parts[m - 1].astype(jnp.float32)
+    lines[mine] = total.astype(jnp.bfloat16)
+    for copy in copies:
+        copy.wait_send()
+    copies = [
+        to_group(m, lines.at[mine], lines.at[mine], line_send, line_recv) for m in masks
+    ]
+    for copy in copies:
+        copy.start()
+    load.wait()
+    for copy in copies:
+        copy.wait()
+
+    left = lines[:, 0].reshape(nb * hours, rank)
+    right = lines[:, 1].reshape(nb * hours, rank)
+    cross[...] = over_hours(left, right).reshape(nb, share, rank)
+    copies = [
+        pltpu.make_async_remote_copy(
+            src_ref=cross.at[mine],
+            dst_ref=planes.at[step - 1],
+            send_sem=plane_send.at[step - 1],
+            recv_sem=plane_recv.at[step - 1],
+            device_id=z_peer(step),
+            device_id_type=MESH,
+        )
+        for step in range(1, nz)
+    ]
+    for copy in copies:
+        copy.start()
+
+    def columns(i, f):
+        cut = pl.ds(pl.multiple_of(i * sub, 128), sub)
+        values = held[f, :, :, cut].reshape(nb * hours, sub)
+        weights = lines[:, 1 - f].reshape(nb * hours, rank)
+        sketch[f, :, cut] = over_hours(weights, values).astype(jnp.bfloat16)
+
+    @pl.loop(0, nz)
+    def _(i):
+        columns(i, 0)
+
+    for copy in copies:
+        copy.wait()
+    ordered = [cross[mine]] + [planes[step - 1] for step in range(1, nz)]
+    summed = jnp.zeros_like(ordered[0])
+    for plane in range(nz):
+        for step in range(nz):
+            summed = summed + jnp.where(lax.rem(z - step + nz, nz) == plane, ordered[step], 0.0)
+    rows[mine] = summed
+    copies = [to_group(m, rows.at[mine], rows.at[mine], row_send, row_recv) for m in masks]
+    for copy in copies:
+        copy.start()
+
+    @pl.loop(0, nz)
+    def _(i):
+        columns(i, 1)
+
+    for copy in copies:
+        copy.wait()
+    middle[...] = rows[...].reshape(rank, rank)
+
+
+def sketches_of(proj, anomaly, nt, nz, sub):
+    nb, _, hours, rank = proj.shape
+    dma = pltpu.SemaphoreType.DMA
+    return pl.pallas_call(
+        functools.partial(sketch_kernel, nt, nz, sub),
+        out_shape=(
+            jax.ShapeDtypeStruct((2, rank, nz * sub), jnp.bfloat16),
+            jax.ShapeDtypeStruct((rank, rank), jnp.float32),
+        ),
+        in_specs=[pl.BlockSpec(memory_space=pltpu.VMEM), pl.BlockSpec(memory_space=pl.ANY)],
+        out_specs=(pl.BlockSpec(memory_space=pltpu.VMEM),) * 2,
+        scratch_shapes=[
+            pltpu.VMEM(anomaly.shape, jnp.bfloat16),
+            pltpu.VMEM((nb - 1, 2, hours, rank), jnp.bfloat16),
+            pltpu.VMEM((nb, 2, hours, rank), jnp.bfloat16),
+            pltpu.VMEM((nb, rank // nb, rank), jnp.float32),
+            pltpu.VMEM((nz - 1, rank // nb, rank), jnp.float32),
+            pltpu.VMEM((nb, rank // nb, rank), jnp.float32),
+            dma,
+            dma((nb - 1,)),
+            dma((nb - 1,)),
+            dma((nb - 1,)),
+            dma((nb - 1,)),
+            dma((nz - 1,)),
+            dma((nz - 1,)),
+            dma((nb - 1,)),
+            dma((nb - 1,)),
+        ],
+        compiler_params=pltpu.CompilerParams(
+            collective_id=1, has_side_effects=True, vmem_limit_bytes=VMEM_LIMIT
+        ),
+        name="sketches",
+    )(proj, anomaly)
+
+
+def split(weights, count):
+    parts = []
+    for _ in range(count):
+        part = lax.reduce_precision(weights, 8, 7)
+        parts.append(part.astype(jnp.bfloat16))
+        weights = weights - part
+    return parts
 
 
 def per_device(warm, wet, fading, starting, warmth_operator, wetness_operator):
@@ -196,14 +366,18 @@
     sub = warm.shape[1] // (nb * nz)
     rank = warmth_operator.shape[1]
 
-    operator = lax.dynamic_slice_in_dim(
-        jnp.stack([warmth_operator, wetness_operator]), t_mine * sub, sub, axis=1
-    )
-    operator = lax.all_gather(operator, "zz", axis=1, tiled=True)
-    start = lax.all_gather(lax.dynamic_slice_in_dim(starting, t_mine * sub, sub, axis=1), "zz")
-    fading = lax.all_gather(fading, "tm", axis=1, tiled=True)
-
-    x = exchange(warm, wet, nt, nz, sub)
+    tile = jnp.stack([warmth_operator, wetness_operator])
+    average = jnp.stack(split(lax.dynamic_slice_in_dim(starting, t_mine * sub, sub, axis=1), 3), 1)
+    average = average.reshape(2, -1, rank)
+    extra = average.shape[1]
+    average = jnp.pad(average, ((0, 0), (0, -extra % 16), (0, 0)))
+    tile = lax.dynamic_slice_in_dim(tile, t_mine * sub, sub, axis=1)
+    tiles = lax.all_gather(jnp.concatenate([tile, average], axis=1), "zz")
+    terms = tiles[:, :, sub : sub + extra].reshape(nz, 2, 3, sub).astype(jnp.float32)
+    start = terms[:, :, 0] + terms[:, :, 1] + terms[:, :, 2]
+
+    x, decays = exchange(warm, wet, fading, nt, nz, sub)
+    fading = jnp.concatenate([decays[2 * t] for t in range(nt)], axis=1)
 
     every = fading.reshape(2, nt, nz, 2, hours)
     gains = jnp.exp(jnp.sum(jnp.log(every), axis=-1)).reshape(2, nt * nz * 2)
@@ -225,21 +399,13 @@
     fade = jnp.exp(exclusive)[..., None]
 
     ends = lax.all_gather(block_ends(to_end, x, sub), "zz")
-    anomaly, proj = anomalies(gains, within, fade, ends, start, x, operator, nt, nz, sub)
-    share = lax.psum_scatter(
-        proj.reshape(2, nb * hours, rank), ("tm", "cc"), scatter_dimension=1, tiled=True
-    ).astype(jnp.bfloat16)
-    lines = lax.all_gather(share, ("tm", "cc"), axis=1, tiled=True)
-    anomaly = anomaly.reshape(2, nb * hours, nz * sub)
+    anomaly, proj = anomalies(gains, within, fade, ends, start, x, tiles, nt, nz, sub)
+    sketches, middle = sketches_of(proj, anomaly, nt, nz, sub)
     scale = (nb * nz * hours) ** (-0.5)
-    sketches = jnp.stack(
-        [over_hours(lines[1], anomaly[0]), over_hours(lines[0], anomaly[1])]
-    ).astype(jnp.bfloat16)
-    middle = lax.psum(over_hours(lines[0], lines[1]), "zz") * scale
     sums = lax.psum_scatter(sketches, "zz", scatter_dimension=2, tiled=True)
     sums = lax.all_to_all(sums, "tm", split_axis=1, concat_axis=2, tiled=True)
     sums = sums.astype(jnp.float32) * scale
-    return sums[0], sums[1], middle
+    return sums[0], sums[1], middle * scale
 
 
 def solution(mesh):

time: 415 us -> 333 us (0.80)
  waiting for transfers between devices: 153 us -> 69.8 us
  Pallas kernels: 164 us -> 205 us
  blocking collectives: 40.5 us -> 20.3 us
  local copies, waits for them, and re-layouts: 20.4 us -> 10.7 us
  matrix products: 7.84 us -> 0 us
    reduce_scatter x1 -> x0, waiting for transfers between devices: 40.9 us -> none  [per_device(): lax.psum_scatter(proj.reshape(2, nb * hours, rank), ('tm', 'cc'), scatter...]
    pallas_call x0 -> x1, Pallas kernels: none -> 40.6 us  [sketches_of(): pl.pallas_call(functools.partial(sketch_kernel, nt, nz, sub), out_shape=(...]
    psum x1 -> x0, waiting for transfers between devices: 38.3 us -> none  [per_device(): middle = lax.psum(over_hours(lines[0], lines[1]), 'zz') * scale]
    all_gather x2 -> x0, blocking collectives: 22.2 us -> none  [the longest x1 14.1 us: per_device(): lax.all_gather(lax.dynamic_slice_in_dim(starting, t_mine * sub, sub, axis...]
    all_gather x2 -> x1, waiting for transfers between devices: 13.6 us -> 0.01 us  [per_device(): tiles = lax.all_gather(jnp.concatenate([tile, average], axis=1), 'zz')]
    slice x4 -> x5, local copies, waits for them, and re-layouts: 13.1 us -> 3.04 us  [the longest x3 2.23 us: per_device(): return (sums[0], sums[1], middle * scale)]
    all_to_all x1, waiting for transfers between devices: 0.01 us -> 10 us  [per_device(): sums = lax.all_to_all(sums, 'tm', split_axis=1, concat_axis=2, tiled=True)]
    dot_general x3 -> x0, matrix products: 7.84 us -> none  [over_hours(): lax.dot_general(left, right, (((0,), (0,)), ((), ())), preferred_element_...]
  transfers between devices with their start and end apart: 6 -> 3, of which waited for: 4 -> 2; matrix products, arithmetic and copies ran while one was open for 5% -> 2% of each run, Pallas kernels for 36% -> 45%
where the time goes in v2:
time: 333 us; the launch traced here: 332 us
  Pallas kernels  205 us (62%)
  waiting for transfers between devices  69.8 us (21%)
  blocking collectives  20.3 us (6%)
  between operations  14.2 us (4%)
  local copies, waits for them, and re-layouts  10.7 us (3%)
  other arithmetic  8.74 us (3%)
  starting transfers between devices  3.75 us (1%)
    pallas_call x1, Pallas kernels, exchange(): pl.pallas_call(functools.partial(exchange_kernel, nt, nz, sub), out_shape...  142 us
    reduce_scatter x1, waiting for transfers between devices, per_device(): sums = lax.psum_scatter(sketches, 'zz', scatter_dimension=2, tiled=True)  59.8 us
    pallas_call x1, Pallas kernels, sketches_of(): pl.pallas_call(functools.partial(sketch_kernel, nt, nz, sub), out_shape=(...  40.6 us
    all_gather x1, blocking collectives, per_device(): ends = lax.all_gather(block_ends(to_end, x, sub), 'zz')  20.3 us
    pallas_call x1, Pallas kernels, anomalies(): pl.pallas_call(functools.partial(anomaly_kernel, nt, nz), grid=(nz,), out...  15.5 us
    all_to_all x1, waiting for transfers between devices, per_device(): sums = lax.all_to_all(sums, 'tm', split_axis=1, concat_axis=2, tiled=True)  10 us
    pallas_call x1, Pallas kernels, block_ends(): pl.pallas_call(ends_kernel, grid=(width // sub,), out_shape=jax.ShapeDtyp...  6.71 us
  transfers between devices with their start and end apart: 3, of which 2 were waited for; matrix products, arithmetic and copies ran while one was open for 2% of the time, Pallas kernels for 45%

profile of v2, /device:TPU:0, one launch (start us, length us, event | category | flops | bytes accessed | tf_op | source)
XLA Modules:
  0.0 332.5 jit_solution(3401042330681030466)
XLA Ops:
  7.2 0.0 all-gather.4.cloned.1.call-start
  7.2 0.7 fusion.16
  8.0 1.2 fusion.4
  9.2 1.0 fusion.3
  10.1 0.0 all-gather.4.cloned.1.call-update
  10.1 0.0 reduce-scatter.2.cloned.1.call-start
  10.2 142.1 %exchange.1 = (bf16[2,8,128,3072]{3,2,1,0:T(8,128)(2,1)}, f32[8,2,1024]{2,1,0:T(2,128)}) custom-call(bf16[128,24576]{1,0:T(8,128)(2,1)} %warm.1, bf16[128,24576]{1,0:T(8,128)(2,1)} %wet.1, f32[2,1024]{1,0:T(2,128)} %fading.1), custom_call_target="tpu_custom_call" | custom-call | flops 99999997952 | bytes 100000000 | tf_op jit(solution)/shard_map/exchange/pallas_call | solution.py:101
  152.3 0.8 fusion.21
  153.2 0.1 fusion.22
  153.4 0.3 select_reduce_fusion
  153.7 0.1 copy.50
  153.9 0.1 copy.51
  154.0 0.7 exp.39.gains
  154.7 0.4 copy.54
  155.1 1.1 exp.41.fade
  156.2 0.2 slice_reduce_fusion
  156.3 0.1 fusion.13
  156.5 0.7 fusion.9.weights
  157.1 6.7 %block_ends.1 = f32[2,8,3072]{2,1,0:T(8,128)} custom-call(bf16[2,8,16,128]{3,2,1,0:T(8,128)(2,1)} %fusion.9.weights, bf16[2,8,128,3072]{3,2,1,0:T(8,128)(2,1)} %get-tuple-element.10.x), custom_call_target="tpu_custom_call" | custom-call | tf_op jit(solution)/shard_map/block_ends/pallas_call | solution.py:131
  163.8 0.0 copy-start
  163.9 0.5 reduce-precision_convert_fusion
  164.3 1.2 pad_maximum_fusion.within
  165.5 0.0 copy-done
  165.5 20.3 %all-gather = f32[8,8,3072]{2,1,0:T(8,128)} all-gather(f32[2,8,3072]{2,1,0:T(8,128)S(1)} %copy-done), channel_id=2, replica_groups=mesh['tm'=4,'zz'=4,'cc'=2] {'zz'}, dimensions={0}, use_global_device_ids=true | all-gather | bytes 983040 | tf_op jit(solution)/shard_map/all_gather | solution.py:401
  185.8 0.0 all-gather.4.cloned.1.call-done
  185.8 0.9 slice_convert_fusion
  186.8 0.1 fusion.20
  186.8 0.6 fusion.10.start
  187.4 15.5 %anomalies.1 = (bf16[2,8,128,3072]{3,2,1,0:T(8,128)(2,1)}, bf16[8,2,128,256]{3,2,1,0:T(8,128)(2,1)}) custom-call(f32[2,32]{1,0:T(2,128)} %exp.39.gains, bf16[2,8,128,256]{3,2,1,0:T(8,128)(2,1)} %pad_maximum_fusion.within, f32[2,8,128,1]{3,2,1,0:T(8,128)} %exp.41.fade, f32[4,2,8,3072]{3,2,1,0:T(8,128)} %bitcast.39, f32[4,2,768]{2,1,0:T(2,128)} %fusion.10.start, ...), custom_call_target="tpu_custom_call" | custom-call | tf_op jit(solution)/shard_map/anomalies/pallas_call | solution.py:180
  203.0 40.6 %sketches.1 = (bf16[2,256,3072]{2,1,0:T(8,128)(2,1)}, f32[256,256]{1,0:T(8,128)}) custom-call(bf16[8,2,128,256]{3,2,1,0:T(8,128)(2,1)} %get-tuple-element.11.proj, bf16[2,8,128,3072]{3,2,1,0:T(8,128)(2,1)} %get-tuple-element.12.anomaly), custom_call_target="tpu_custom_call" | custom-call | tf_op jit(solution)/shard_map/sketches/pallas_call | solution.py:320
  243.6 0.0 reduce-scatter.2.cloned.1.call-update
  243.6 0.0 copy-start.1
  243.6 59.8 %reduce-scatter.2.cloned.1.call-done = bf16[2,256,768]{2,1,0:T(8,128)(2,1)} async-done(((bf16[2,256,3072]{2,1,0:T(8,128)(2,1)}), bf16[2,256,768]{2,1,0:T(8,128)(2,1)}) %reduce-scatter.2.cloned.1.call-update) | async-done | bytes 786448 | tf_op jit(solution)/shard_map/reduce_scatter | solution.py:405
  303.4 2.8 copy.60
  306.2 3.7 %all-to-all-start = ((bf16[2,256,768]{2,0,1:T(2,128)(2,1)}), bf16[2,256,768]{2,0,1:T(2,128)(2,1)S(1)}, u32[]{:S(2)}, u32[]{:S(2)}) async-start(bf16[2,256,768]{2,0,1:T(2,128)(2,1)} %copy.60), calls=%async_computation.1 | async-start | bytes 1572864 | tf_op jit(solution)/shard_map/all_to_all | solution.py:406
  309.9 0.0 copy-done.1
  309.9 0.7 broadcast_multiply_fusion
  310.7 10.0 %all-to-all-done = bf16[2,256,768]{2,0,1:T(2,128)(2,1)S(1)} async-done(((bf16[2,256,768]{2,0,1:T(2,128)(2,1)}), bf16[2,256,768]{2,0,1:T(2,128)(2,1)S(1)}, u32[]{:S(2)}, u32[]{:S(2)}) %all-to-all-start) | async-done | bytes 786464 | tf_op jit(solution)/shard_map/all_to_all | solution.py:406
  320.7 0.7 convert_multiply_fusion
  321.4 1.2 fusion.19
  322.6 0.5 copy.62
  323.1 1.0 copy.68
  324.1 0.5 copy.61
  324.6 1.0 copy.67
  (15 shorter events, 0.3 us)
Async XLA Ops:
  7.2 178.7 %all-gather.4.cloned.1.call-start = ((), (), s32[]{:S(2)}) async-start(), calls=%async_computation.3 | async-start | bytes 4014080 | tf_op jit(solution)/shard_map/all_gather | solution.py:375
  10.1 293.3 %reduce-scatter.2.cloned.1.call-start = ((), (), s32[]{:S(2)}) async-start(), calls=%async_computation.2 | async-start | bytes 3932160 | tf_op jit(solution)/shard_map/reduce_scatter | solution.py:405
  163.8 1.7 copy-start
  243.6 66.3 %copy-start.1 = (f32[256,256]{1,0:T(8,128)S(1)}, f32[256,256]{1,0:T(8,128)}, u32[]{:S(2)}) copy-start(f32[256,256]{1,0:T(8,128)} %get-tuple-element.14) | copy-start | bytes 786436
  306.2 14.4 %all-to-all-start = ((bf16[2,256,768]{2,0,1:T(2,128)(2,1)}), bf16[2,256,768]{2,0,1:T(2,128)(2,1)S(1)}, u32[]{:S(2)}, u32[]{:S(2)}) async-start(bf16[2,256,768]{2,0,1:T(2,128)(2,1)} %copy.60), calls=%async_computation.1 | async-start | bytes 1572864 | tf_op jit(solution)/shard_map/all_to_all | solution.py:406
Sparse Core Ops, SparseCore 0:
  10.3 67.2 all-gather.3
  243.8 59.6 reduce-scatter.1

commit v3 on v2

--- a/solution.py
+++ b/solution.py
@@ -142,7 +142,7 @@
     )(weights, x)
 
 
-def anomaly_kernel(nt, nz, gains, within, fade, ends, start, x, operator, anomaly, proj, total):
+def anomaly_kernel(nt, nz, gains, within, fade, ends, own, start, x, operator, anomaly, proj, total):
     nb = nt * 2
     z_mine = lax.axis_index("zz")
 
@@ -155,11 +155,13 @@
         entering = [level] * nb
         for t in range(nt):
             for z in range(nz):
-                for c in range(2):
-                    b = t * 2 + c
-                    entering[b] = jnp.where(z_mine == z, level, entering[b])
-                    step = (t * nz + z) * 2 + c
-                    level = gains[f, step] * level + ends[z, f, b : b + 1, :]
+                step = t * nz + z
+                entering[t * 2] = jnp.where(z_mine == z, level, entering[t * 2])
+                level = (
+                    gains[f, step * 2] * gains[f, step * 2 + 1] * level + ends[z, f, t : t + 1, :]
+                )
+            first = gains[f, (t * nz + z_mine) * 2]
+            entering[t * 2 + 1] = first * entering[t * 2] + own[f, t * 2 : t * 2 + 1, :]
         for b in range(nb):
             values = x[f, b]
             twice = jnp.concatenate([values, values], axis=0)
@@ -174,7 +176,7 @@
         proj[...] = total[...].astype(proj.dtype)
 
 
-def anomalies(gains, within, fade, ends, start, x, operator, nt, nz, sub):
+def anomalies(gains, within, fade, ends, own, start, x, operator, nt, nz, sub):
     _, nb, hours, width = x.shape
     rank = operator.shape[-1]
     return pl.pallas_call(
@@ -188,7 +190,8 @@
             pl.BlockSpec(memory_space=pltpu.SMEM),
             pl.BlockSpec(within.shape, lambda i: (0, 0, 0, 0)),
             pl.BlockSpec(fade.shape, lambda i: (0, 0, 0, 0)),
-            pl.BlockSpec((nz, 2, nb, sub), lambda i: (0, 0, 0, i)),
+            pl.BlockSpec((nz, 2, nt, sub), lambda i: (0, 0, 0, i)),
+            pl.BlockSpec((2, nb, sub), lambda i: (0, 0, i)),
             pl.BlockSpec((1, 2, sub), lambda i: (i, 0, 0)),
             pl.BlockSpec((2, nb, hours, sub), lambda i: (0, 0, 0, i)),
             pl.BlockSpec((1, 2, sub, rank), lambda i: (i, 0, 0, 0)),
@@ -200,7 +203,7 @@
         scratch_shapes=[pltpu.VMEM((nb, 2, hours, rank), jnp.float32)],
         compiler_params=pltpu.CompilerParams(vmem_limit_bytes=VMEM_LIMIT),
         name="anomalies",
-    )(gains, within, fade, ends, start, x, operator)
+    )(gains, within, fade, ends, own, start, x, operator)
 
 
 def over_hours(left, right):
@@ -398,8 +401,11 @@
     to_end = jnp.pad(to_end, ((0, 0), (0, 0), (0, 13), (0, 0)))
     fade = jnp.exp(exclusive)[..., None]
 
-    ends = lax.all_gather(block_ends(to_end, x, sub), "zz")
-    anomaly, proj = anomalies(gains, within, fade, ends, start, x, tiles, nt, nz, sub)
+    own = block_ends(to_end, x, sub)
+    pairs = own.reshape(2, nt, 2, nz * sub)
+    second = jnp.exp(inclusive[..., -1]).reshape(2, nt, 2)[:, :, 1, None]
+    ends = lax.all_gather(second * pairs[:, :, 0] + pairs[:, :, 1], "zz")
+    anomaly, proj = anomalies(gains, within, fade, ends, own, start, x, tiles, nt, nz, sub)
     sketches, middle = sketches_of(proj, anomaly, nt, nz, sub)
     scale = (nb * nz * hours) ** (-0.5)
     sums = lax.psum_scatter(sketches, "zz", scatter_dimension=2, tiled=True)

time: 333 us -> 330 us (level)
  blocking collectives: 20.3 us -> 15.4 us
    all_gather x1, blocking collectives: 20.3 us -> 15.4 us  [per_device(): ends = lax.all_gather(second * pairs[:, :, 0] + pairs[:, :, 1], 'zz')]
  transfers between devices with their start and end apart: 3 -> 3, of which waited for: 2 -> 2; matrix products, arithmetic and copies ran while one was open for 2% -> 3% of each run, Pallas kernels for 45% -> 45%
where the time goes in v3:
time: 330 us
  Pallas kernels  207 us (63%)
  waiting for transfers between devices  68.6 us (21%)
  blocking collectives  15.4 us (5%)
  between operations  14.3 us (4%)
  local copies, waits for them, and re-layouts  12 us (4%)
  other arithmetic  8.84 us (3%)
  starting transfers between devices  3.75 us (1%)
    pallas_call x1, Pallas kernels, exchange(): pl.pallas_call(functools.partial(exchange_kernel, nt, nz, sub), out_shape...  142 us
    reduce_scatter x1, waiting for transfers between devices, per_device(): sums = lax.psum_scatter(sketches, 'zz', scatter_dimension=2, tiled=True)  58.6 us
    pallas_call x1, Pallas kernels, sketches_of(): pl.pallas_call(functools.partial(sketch_kernel, nt, nz, sub), out_shape=(...  42.6 us
    pallas_call x1, Pallas kernels, anomalies(): pl.pallas_call(functools.partial(anomaly_kernel, nt, nz), grid=(nz,), out...  15.4 us
    all_gather x1, blocking collectives, per_device(): ends = lax.all_gather(second * pairs[:, :, 0] + pairs[:, :, 1], 'zz')  15.4 us
    all_to_all x1, waiting for transfers between devices, per_device(): sums = lax.all_to_all(sums, 'tm', split_axis=1, concat_axis=2, tiled=True)  9.99 us
    pallas_call x1, Pallas kernels, block_ends(): pl.pallas_call(ends_kernel, grid=(width // sub,), out_shape=jax.ShapeDtyp...  6.69 us
  transfers between devices with their start and end apart: 3, of which 2 were waited for; matrix products, arithmetic and copies ran while one was open for 3% of the time, Pallas kernels for 45%

profile of v3, /device:TPU:0, one launch (start us, length us, event | category | flops | bytes accessed | tf_op | source)
XLA Modules:
  0.0 329.7 jit_solution(497543322028045673)
XLA Ops:
  7.2 0.0 all-gather.3.cloned.1.call-start
  7.2 0.7 fusion.18
  8.0 1.2 fusion.4
  9.2 1.0 fusion.3
  10.1 0.0 all-gather.3.cloned.1.call-update
  10.1 0.0 reduce-scatter.2.cloned.1.call-start
  10.2 142.1 %exchange.1 = (bf16[2,8,128,3072]{3,2,1,0:T(8,128)(2,1)}, f32[8,2,1024]{2,1,0:T(2,128)}) custom-call(bf16[128,24576]{1,0:T(8,128)(2,1)} %warm.1, bf16[128,24576]{1,0:T(8,128)(2,1)} %wet.1, f32[2,1024]{1,0:T(2,128)} %fading.1), custom_call_target="tpu_custom_call" | custom-call | flops 99999997952 | bytes 100000000 | tf_op jit(solution)/shard_map/exchange/pallas_call | solution.py:101
  152.3 0.8 fusion.23
  153.2 0.1 fusion.24
  153.4 0.3 select_reduce_fusion
  153.7 0.2 exponential_reduce_fusion
  153.9 0.1 exp.50
  154.0 0.1 slice.60
  154.0 0.1 copy.75
  154.2 0.1 copy.57
  154.3 0.1 copy.58
  154.4 0.7 exp.46.gains
  155.1 0.1 fusion.15
  155.2 0.7 fusion.11.weights
  155.9 6.7 %block_ends.1.own = f32[2,8,3072]{2,1,0:T(8,128)} custom-call(bf16[2,8,16,128]{3,2,1,0:T(8,128)(2,1)} %fusion.11.weights, bf16[2,8,128,3072]{3,2,1,0:T(8,128)(2,1)} %get-tuple-element.10.x), custom_call_target="tpu_custom_call" | custom-call | tf_op jit(solution)/shard_map/block_ends/pallas_call | solution.py:131
  162.6 1.1 copy.64
  163.7 0.1 fusion.8
  163.8 0.4 copy.61
  164.2 1.1 exp.48.fade
  165.4 0.5 reduce-precision_convert_fusion
  165.8 1.2 pad_maximum_fusion.within
  167.1 15.4 %all_gather.10.ends = f32[4,2,4,3072]{3,2,1,0:T(4,128)} all-gather(f32[1,2,4,3072]{3,2,1,0:T(4,128)S(1)} %copy.66), channel_id=1, replica_groups=mesh['tm'=4,'zz'=4,'cc'=2] {'zz'}, dimensions={0}, use_global_device_ids=true | all-gather | bytes 491520 | tf_op jit(solution)/shard_map/all_gather | solution.py:407
  182.4 0.0 all-gather.3.cloned.1.call-done
  182.4 0.9 slice_convert_fusion
  183.3 0.1 fusion.22
  183.4 0.6 fusion.12.start
  184.0 15.4 %anomalies.1 = (bf16[2,8,128,3072]{3,2,1,0:T(8,128)(2,1)}, bf16[8,2,128,256]{3,2,1,0:T(8,128)(2,1)}) custom-call(f32[2,32]{1,0:T(2,128)} %exp.46.gains, bf16[2,8,128,256]{3,2,1,0:T(8,128)(2,1)} %pad_maximum_fusion.within, f32[2,8,128,1]{3,2,1,0:T(8,128)} %exp.48.fade, f32[4,2,4,3072]{3,2,1,0:T(4,128)} %all_gather.10.ends, f32[2,8,3072]{2,1,0:T(8,128)} %block_ends.1.own, ...), custom_call_target="tpu_custom_call" | custom-call | tf_op jit(solution)/shard_map/anomalies/pallas_call | solution.py:182
  199.5 42.6 %sketches.1 = (bf16[2,256,3072]{2,1,0:T(8,128)(2,1)}, f32[256,256]{1,0:T(8,128)}) custom-call(bf16[8,2,128,256]{3,2,1,0:T(8,128)(2,1)} %get-tuple-element.11.proj, bf16[2,8,128,3072]{3,2,1,0:T(8,128)(2,1)} %get-tuple-element.12.anomaly), custom_call_target="tpu_custom_call" | custom-call | tf_op jit(solution)/shard_map/sketches/pallas_call | solution.py:323
  242.1 0.0 reduce-scatter.2.cloned.1.call-update
  242.1 0.0 copy-start
  242.1 58.6 %reduce-scatter.2.cloned.1.call-done = bf16[2,256,768]{2,1,0:T(8,128)(2,1)} async-done(((bf16[2,256,3072]{2,1,0:T(8,128)(2,1)}), bf16[2,256,768]{2,1,0:T(8,128)(2,1)}) %reduce-scatter.2.cloned.1.call-update) | async-done | bytes 786448 | tf_op jit(solution)/shard_map/reduce_scatter | solution.py:411
  300.7 2.8 copy.71
  303.5 3.7 %all-to-all-start = ((bf16[2,256,768]{2,0,1:T(2,128)(2,1)}), bf16[2,256,768]{2,0,1:T(2,128)(2,1)S(1)}, u32[]{:S(2)}, u32[]{:S(2)}) async-start(bf16[2,256,768]{2,0,1:T(2,128)(2,1)} %copy.71), calls=%async_computation.1 | async-start | bytes 1572864 | tf_op jit(solution)/shard_map/all_to_all | solution.py:412
  307.2 0.0 copy-done
  307.2 0.7 broadcast_multiply_fusion
  307.9 10.0 %all-to-all-done = bf16[2,256,768]{2,0,1:T(2,128)(2,1)S(1)} async-done(((bf16[2,256,768]{2,0,1:T(2,128)(2,1)}), bf16[2,256,768]{2,0,1:T(2,128)(2,1)S(1)}, u32[]{:S(2)}, u32[]{:S(2)}) %all-to-all-start) | async-done | bytes 786464 | tf_op jit(solution)/shard_map/all_to_all | solution.py:412
  317.9 0.7 convert_multiply_fusion
  318.6 1.2 fusion.21
  319.8 0.5 copy.73
  320.3 1.0 copy.81
  321.3 0.5 copy.72
  321.8 1.0 copy.80
  (16 shorter events, 0.3 us)
Async XLA Ops:
  7.2 175.2 %all-gather.3.cloned.1.call-start = ((), (), s32[]{:S(2)}) async-start(), calls=%async_computation.3 | async-start | bytes 4014080 | tf_op jit(solution)/shard_map/all_gather | solution.py:378
  10.1 290.5 %reduce-scatter.2.cloned.1.call-start = ((), (), s32[]{:S(2)}) async-start(), calls=%async_computation.2 | async-start | bytes 3932160 | tf_op jit(solution)/shard_map/reduce_scatter | solution.py:411
  242.1 65.1 %copy-start = (f32[256,256]{1,0:T(8,128)S(1)}, f32[256,256]{1,0:T(8,128)}, u32[]{:S(2)}) copy-start(f32[256,256]{1,0:T(8,128)} %get-tuple-element.14) | copy-start | bytes 786436
  303.5 14.4 %all-to-all-start = ((bf16[2,256,768]{2,0,1:T(2,128)(2,1)}), bf16[2,256,768]{2,0,1:T(2,128)(2,1)S(1)}, u32[]{:S(2)}, u32[]{:S(2)}) async-start(bf16[2,256,768]{2,0,1:T(2,128)(2,1)} %copy.71), calls=%async_computation.1 | async-start | bytes 1572864 | tf_op jit(solution)/shard_map/all_to_all | solution.py:412
Sparse Core Ops, SparseCore 0:
  10.3 67.2 all-gather.2
  242.2 58.4 reduce-scatter.1
